TPU v7x, 32 devices: a whole 2x2x4 slice. The times are simulated.
32 devices in a mesh: dp: 8 (over z, y), mp: 4 (over x, core).
Axes of the slice: x: 2, y: 2, z: 4, core: 2. Of those that a mesh axis runs over, the one named last changes fastest.
Arguments:
- images: bfloat16 [256, 196, 768], P(('dp', 'mp')), may hold values from -6 to 6
- kept_mask: int32 [256, 196], P(('dp', 'mp')), may hold values from 0 to 1, as said below
- pooled_grad: float32 [256, 768], P(('dp', 'mp')), may hold values from -600 to 600
- token_weights: float32 [2, 196, 384], P(None, None, 'dp'), may hold values from -0.4375 to 0.4375
- norm_gain: float32 [2, 768], replicated, may hold values from 0.5 to 1.5
- norm_bias: float32 [2, 768], replicated, may hold values from -1.8 to 1.8
- mixing_bias: float32 [384], replicated, may hold values from -1.8 to 1.8
- patch_bias: float32 [196], replicated, may hold values from -1.8 to 1.8
- widening: float32 [768, 3072], P('dp', 'mp'), may hold values from -0.21875 to 0.21875
- narrowing: float32 [3072, 768], P('mp', 'dp'), may hold values from -0.109375 to 0.109375
- hidden_bias: float32 [3072], replicated, may hold values from -1.8 to 1.8
- output_bias: float32 [768], replicated, may hold values from -1.8 to 1.8
- width_maps: bfloat16 [2, 768, 64], replicated, may hold values from -0.21875 to 0.21875
- hidden_maps: bfloat16 [2, 3072, 64], P(None, 'mp'), may hold values from -0.109375 to 0.109375
- queries: bfloat16 [256, 162176], P(None, 'dp'), may hold values from -0.015625 to 0.015625
Outputs:
- pooled: float32 [256, 768], P(('dp', 'mp'))
- image_grad: float32 [256, 196, 768], P(('dp', 'mp'))
- token_grad: float32 [2, 196, 384], P(None, None, 'dp')
- gain_grad: float32 [2, 768], replicated
- shift_grad: float32 [2, 768], replicated
- mixing_grad: float32 [384], replicated
- patch_grad: float32 [196], replicated
- widening_grad: float32 [768, 3072], P('dp', 'mp')
- narrowing_grad: float32 [3072, 768], P('mp', 'dp')
- hidden_grad: float32 [3072], replicated
- output_grad: float32 [768], replicated
- influence: float32 [256, 256], P(('dp', 'mp'))
Inputs may be any that keep to these rules, and one draw needn't show every extreme that they name: `kept_mask`: every image keeps at least 49 of its patches.
All inputs are finite; a program needn't handle non-finite values.
Results may differ from a plain program's by a relative error of at most 0.012.
Values may be sent and summed in bfloat16 or wider, within the bound.
No kernel may reach another device: no remote copies, remote signals or barrier semaphores. Data moves between devices by JAX's collectives and lax.ppermute only.
A program may use at most 320 MiB of HBM per device.

v0:
```python
import jax
import jax.numpy as jnp
from jax import lax
from jax.sharding import PartitionSpec as P

norm_eps = 1e-06


def split_up(array, dim, devices):
    before, after = (array.shape[:dim], array.shape[dim + 1 :])
    return jnp.moveaxis(array.reshape(*before, devices, -1, *after), dim, 0)


def summed_on_arrival(array, axis, dim):
    parts = split_up(array, dim, lax.axis_size(axis))
    arrived = lax.all_to_all(parts, axis, split_axis=0, concat_axis=0, tiled=True)
    return arrived.astype(jnp.float32).sum(axis=0)


def normalize(values):
    average = jnp.mean(values, axis=-1, keepdims=True)
    centered = values - average
    spread = jnp.mean(centered * centered, axis=-1, keepdims=True)
    inverse = lax.rsqrt(spread + norm_eps)
    return (centered * inverse, inverse)


def norm_back(grad_norm, normed, inverse):
    first_mean = jnp.mean(grad_norm, axis=-1, keepdims=True)
    second_mean = jnp.mean(grad_norm * normed, axis=-1, keepdims=True)
    return inverse * (grad_norm - first_mean - normed * second_mean)


def gelu_slope(values):
    cumulative = 0.5 * (1.0 + lax.erf(values * 0.7071067811865476))
    density = jnp.exp(-0.5 * values * values) * 0.3989422804014327
    return cumulative + values * density


def matmul(left, right):
    return jnp.dot(left, right, preferred_element_type=jnp.float32)


def contract_rows(left, right):
    return lax.dot_general(
        left, right, (((0,), (0,)), ((), ())), preferred_element_type=jnp.float32
    )


def contract_cols(left, right):
    return lax.dot_general(
        left, right, (((1,), (1,)), ((), ())), preferred_element_type=jnp.float32
    )


def channel_forward(second_rows, widen_mat, narrow_mat, bias_vec):
    pre_hidden = matmul(second_rows, widen_mat) + bias_vec
    chan_hidden = jax.nn.gelu(pre_hidden, approximate=False).astype(jnp.bfloat16)
    return (pre_hidden, chan_hidden, matmul(chan_hidden, narrow_mat))


def channel_backward(
    second_rows,
    pre_hidden,
    chan_hidden,
    grad_rows,
    widen_mat,
    narrow_mat,
    width_maps,
    hidden_maps,
    patches,
):
    narrow_grad = contract_rows(chan_hidden, grad_rows)
    hidden_back = contract_cols(grad_rows, narrow_mat)
    pre_grad = (hidden_back * gelu_slope(pre_hidden)).astype(jnp.bfloat16)
    bias_sum = jnp.sum(pre_grad.astype(jnp.float32), axis=0)
    widen_grad = contract_rows(second_rows, pre_grad)
    second_grad = contract_cols(pre_grad, widen_mat)
    image_rows = second_rows.shape[0] // patches
    adapter_rank = width_maps.shape[2]
    left_in = matmul(second_rows, width_maps[0]).reshape(image_rows, patches, adapter_rank)
    right_in = matmul(pre_grad, hidden_maps[0]).reshape(image_rows, patches, adapter_rank)
    left_out = matmul(chan_hidden, hidden_maps[1]).reshape(image_rows, patches, adapter_rank)
    right_out = matmul(grad_rows, width_maps[1]).reshape(image_rows, patches, adapter_rank)
    adapter_in = jnp.einsum("npr,nps->nrs", left_in, right_in, precision=lax.Precision.HIGHEST)
    adapter_out = jnp.einsum("npr,nps->nrs", left_out, right_out, precision=lax.Precision.HIGHEST)
    return (
        widen_grad,
        narrow_grad,
        bias_sum,
        second_grad,
        jnp.stack([adapter_in, adapter_out], axis=1),
    )


def body(
    images,
    kept_mask,
    pooled_grad,
    token_weights,
    norm_gain,
    norm_bias,
    mixing_bias,
    patch_bias,
    widening,
    narrowing,
    hidden_bias,
    output_bias,
    width_maps,
    hidden_maps,
    queries,
):
    image_count, patches, features = images.shape
    token_low, widen_part, narrow_part = (
        lax.all_gather(token_weights.astype(jnp.bfloat16), "dp", axis=2, tiled=True),
        lax.all_gather(widening.astype(jnp.bfloat16), "dp", axis=0, tiled=True),
        lax.all_gather(narrowing.astype(jnp.bfloat16), "dp", axis=1, tiled=True),
    )
    inputs_f = images.astype(jnp.float32)
    keep_f = kept_mask.astype(jnp.float32)[:, :, None]
    kept_count = jnp.sum(keep_f, axis=1)
    normed_one, inverse_one = normalize(inputs_f)
    first_norm = normed_one * norm_gain[0] + norm_bias[0]
    masked = (first_norm * keep_f).astype(jnp.bfloat16)
    mixed_in = (
        jnp.einsum("bpc,pj->bcj", masked, token_low[0], preferred_element_type=jnp.float32)
        + mixing_bias
    )
    token_hidden = jax.nn.gelu(mixed_in, approximate=False).astype(jnp.bfloat16)
    mixed_out = jnp.einsum(
        "bcj,pj->bpc", token_hidden, token_low[1], preferred_element_type=jnp.float32
    )
    residual = inputs_f + mixed_out + patch_bias[:, None]
    normed_two, inverse_two = normalize(residual)
    second = (normed_two * norm_gain[1] + norm_bias[1]).astype(jnp.bfloat16)
    block_grad = keep_f * (pooled_grad / kept_count)[:, None, :]
    block_low = block_grad.astype(jnp.bfloat16)
    model_rank = lax.axis_index("mp")
    hidden_part = widen_part.shape[1]
    bias_part = lax.dynamic_slice_in_dim(hidden_bias, model_rank * hidden_part, hidden_part)
    second_group = lax.all_gather(second, "mp", axis=0, tiled=True)
    group_flat = second_group.reshape(-1, features)
    pre_hidden, chan_hidden, partial_out = channel_forward(
        group_flat, widen_part, narrow_part, bias_part
    )
    channel_out = lax.psum_scatter(
        partial_out.reshape(-1, patches, features).astype(jnp.bfloat16),
        "mp",
        scatter_dimension=0,
        tiled=True,
    ).astype(jnp.float32)
    grad_group = lax.all_gather(block_low, "mp", axis=0, tiled=True)
    widen_share, narrow_share, hidden_sum, second_back, adapter_part = channel_backward(
        group_flat,
        pre_hidden,
        chan_hidden,
        grad_group.reshape(-1, features),
        widen_part,
        narrow_part,
        width_maps,
        hidden_maps,
        patches,
    )
    second_grad, adapter_grad = (
        lax.psum_scatter(
            second_back.reshape(-1, patches, features).astype(jnp.bfloat16),
            "mp",
            scatter_dimension=0,
            tiled=True,
        ).astype(jnp.float32),
        lax.psum_scatter(
            adapter_part.astype(jnp.bfloat16), "mp", scatter_dimension=0, tiled=True
        ).astype(jnp.float32),
    )
    hidden_total = lax.dynamic_update_slice_in_dim(
        jnp.zeros(hidden_bias.shape, jnp.float32), hidden_sum, model_rank * hidden_part, 0
    )
    block_out = residual + channel_out + output_bias
    pooled = jnp.sum(block_out * keep_f, axis=1) / kept_count
    output_sum = jnp.sum(block_low.astype(jnp.float32), axis=(0, 1))
    residual_grad = block_grad + norm_back(second_grad * norm_gain[1], normed_two, inverse_two)
    gain_two = jnp.sum(second_grad * normed_two, axis=1)
    shift_two = jnp.sum(second_grad, axis=1)
    mixing_low = residual_grad.astype(jnp.bfloat16)
    patch_sum = jnp.sum(mixing_low.astype(jnp.float32), axis=(0, 2))
    outward_each = jnp.einsum(
        "bpc,bcj->bpj", mixing_low, token_hidden, preferred_element_type=jnp.float32
    )
    token_hidden_grad = jnp.einsum(
        "bpc,pj->bcj", mixing_low, token_low[1], preferred_element_type=jnp.float32
    )
    mixed_in_grad = (token_hidden_grad * gelu_slope(mixed_in)).astype(jnp.bfloat16)
    mixing_each = jnp.sum(mixed_in_grad.astype(jnp.float32), axis=1)
    inward_each = jnp.einsum(
        "bpc,bcj->bpj", masked, mixed_in_grad, preferred_element_type=jnp.float32
    )
    masked_grad = jnp.einsum(
        "bcj,pj->bpc", mixed_in_grad, token_low[0], preferred_element_type=jnp.float32
    )
    first_grad = masked_grad * keep_f
    gain_one = jnp.sum(first_grad * normed_one, axis=1)
    shift_one = jnp.sum(first_grad, axis=1)
    image_grad = residual_grad + norm_back(first_grad * norm_gain[0], normed_one, inverse_one)
    token_each = jnp.stack([inward_each, outward_each], axis=1)
    gain_each = jnp.stack([gain_one, gain_two], axis=1)
    shift_each = jnp.stack([shift_one, shift_two], axis=1)
    vector = jnp.concatenate(
        [
            token_each.reshape(image_count, -1),
            mixing_each,
            gain_each.reshape(image_count, -1),
            shift_each.reshape(image_count, -1),
            adapter_grad.reshape(image_count, -1),
        ],
        axis=1,
    ).astype(jnp.bfloat16)
    received = lax.all_to_all(vector, "dp", split_axis=1, concat_axis=0, tiled=True)
    partial_scores = contract_cols(received, queries)
    influence = lax.psum_scatter(partial_scores, "dp", scatter_dimension=0, tiled=True)
    widening_grad, narrowing_grad, token_share = (
        summed_on_arrival(widen_share.astype(jnp.bfloat16), "dp", 0),
        summed_on_arrival(narrow_share.astype(jnp.bfloat16), "dp", 1),
        summed_on_arrival(jnp.sum(token_each, axis=0).astype(jnp.bfloat16), "dp", 2),
    )
    token_grad = lax.psum(token_share, "mp")
    gain_grad, shift_grad, mixing_grad, patch_grad, hidden_grad, output_grad = lax.psum(
        (
            jnp.sum(gain_each, axis=0),
            jnp.sum(shift_each, axis=0),
            jnp.sum(mixing_each, axis=0),
            patch_sum,
            hidden_total,
            output_sum,
        ),
        ("dp", "mp"),
    )
    return (
        pooled,
        image_grad,
        token_grad,
        gain_grad,
        shift_grad,
        mixing_grad,
        patch_grad,
        widening_grad,
        narrowing_grad,
        hidden_grad,
        output_grad,
        influence,
    )


def solution(mesh):
    placed = (
        P(("dp", "mp"), None, None),
        P(("dp", "mp"), None),
        P(("dp", "mp"), None),
        P(None, None, "dp"),
        P(),
        P(),
        P(),
        P(),
        P("dp", "mp"),
        P("mp", "dp"),
        P(),
        P(),
        P(),
        P(None, "mp", None),
        P(None, "dp"),
    )
    return jax.shard_map(
        body,
        mesh=mesh,
        in_specs=placed,
        out_specs=(
            P(("dp", "mp"), None),
            P(("dp", "mp"), None, None),
            P(None, None, "dp"),
            P(),
            P(),
            P(),
            P(),
            P("dp", "mp"),
            P("mp", "dp"),
            P(),
            P(),
            P(("dp", "mp"), None),
        ),
        check_vma=False,
    )
```

profile of v0, /device:TPU:0, one launch (start us, length us, event | category | flops | bytes accessed | tf_op | source)
XLA Modules:
  0.0 789.0 jit_solution(6513889651765379230)
XLA Ops:
  15.6 32.7 %all_gather.15 = bf16[2,196,384]{1,0,2:T(2,128)(2,1)S(1)} all-gather(bf16[2,196,48]{1,0,2:T(2,128)(2,1)S(1)} %copy.107), channel_id=1, replica_groups=mesh['dp'=8,'mp'=4] {'dp'}, dimensions={2}, use_global_device_ids=true | all-gather | bytes 338688 | tf_op jit(solution)/shard_map/all_gather | solution.py:115
  57.9 21.5 %fusion.18 = bf16[8,768,384]{2,1,0:T(8,128)(2,1)S(1)} fusion(f32[8,768,384]{2,1,0:T(8,128)S(1)} %get-tuple-element.86, f32[384]{0:T(512)S(1)} %copy-done.43, u8[768,384]{1,0:T(8,128)(4,1)S(1)} %get-tuple-element.61, u8[768,384]{1,0:T(8,128)(4,1)S(1)} %get-tuple-element.60), kind=kLoop, calls=%fused_computation.33 | loop fusion | flops 167510016 | bytes 14747136 | tf_op jit(solution)/shard_map/convert_element_type | solution.py:129
  92.9 60.8 %all-gather.5.cloned.1.call-done = bf16[32,196,768]{2,0,1:T(8,128)(2,1)} async-done(((bf16[8,196,768]{2,0,1:T(8,128)(2,1)}), bf16[32,196,768]{2,0,1:T(8,128)(2,1)}) %all-gather.5.cloned.1.call-update) | async-done | bytes 9633808 | tf_op jit(solution)/shard_map/all_gather | solution.py:141
  153.7 12.9 %copy.57 = bf16[32,196,768]{2,1,0:T(8,128)(2,1)} copy(bf16[32,196,768]{2,0,1:T(8,128)(2,1)} %all-gather.5.cloned.1.call-done) | data formatting | bytes 19267584 | tf_op jit(solution)/shard_map/all_gather | solution.py:141
  166.7 13.5 %reshape.126 = bf16[6272,768]{1,0:T(8,128)(2,1)} reshape(bf16[32,196,768]{2,1,0:T(8,128)(2,1)} %copy.57) | data formatting | bytes 19267584 | tf_op jit(solution)/shard_map/reshape | solution.py:142
  180.2 16.8 %all-gather.7.cloned.1.call-done = bf16[768,768]{1,0:T(8,128)(2,1)} async-done(((bf16[96,768]{1,0:T(8,128)(2,1)}), bf16[768,768]{1,0:T(8,128)(2,1)}) %all-gather.7.cloned.1.call-update) | async-done | bytes 1179664 | tf_op jit(solution)/shard_map/all_gather | solution.py:116
  197.0 50.5 %fusion.2 = (bf16[6272,768]{1,0:T(8,128)(2,1)}, f32[6272,768]{1,0:T(8,128)}) fusion(f32[768]{0:T(1024)S(1)} %dynamic_slice.3, bf16[6272,768]{1,0:T(8,128)(2,1)} %reshape.126, bf16[768,768]{1,0:T(8,128)(2,1)} %all-gather.7.cloned.1.call-done), kind=kOutput, calls=%fused_computation.4 | convolution fusion | flops 7716667392 | bytes 39717888 | tf_op jit(solution)/shard_map/dot_general | solution.py:41
  247.5 15.2 %all-gather.11.cloned.1.call-done = bf16[32,196,768]{2,0,1:T(8,128)(2,1)} async-done(((bf16[8,196,768]{2,0,1:T(8,128)(2,1)}), bf16[32,196,768]{2,0,1:T(8,128)(2,1)}) %all-gather.11.cloned.1.call-update) | async-done | bytes 9633808 | tf_op jit(solution)/shard_map/all_gather | solution.py:152
  262.7 12.9 %copy.59 = bf16[32,196,768]{2,1,0:T(8,128)(2,1)} copy(bf16[32,196,768]{2,0,1:T(8,128)(2,1)} %all-gather.11.cloned.1.call-done) | data formatting | bytes 19267584 | tf_op jit(solution)/shard_map/all_gather | solution.py:152
  275.6 13.1 %reshape.127 = bf16[6272,768]{1,0:T(8,128)(2,1)} reshape(bf16[32,196,768]{2,1,0:T(8,128)(2,1)} %copy.59) | data formatting | bytes 19267584 | tf_op jit(solution)/shard_map/reshape | solution.py:157
  288.7 17.1 %all-gather.9.cloned.1.call-done = bf16[768,768]{0,1:T(8,128)(2,1)} async-done(((bf16[768,96]{0,1:T(8,128)(2,1)}), bf16[768,768]{0,1:T(8,128)(2,1)}) %all-gather.9.cloned.1.call-update) | async-done | bytes 1179664 | tf_op jit(solution)/shard_map/all_gather | solution.py:117
  305.9 17.4 %convert_reduce_fusion = (f32[768]{0:T(1024)}, bf16[6272,768]{1,0:T(8,128)(2,1)S(1)}) fusion(f32[6272,768]{1,0:T(8,128)} %get-tuple-element.90, f32[768]{0:T(1024)S(1)} %dynamic_slice.3, bf16[6272,768]{1,0:T(8,128)(2,1)} %reshape.127, bf16[768,768]{0,1:T(8,128)(2,1)} %all-gather.9.cloned.1.call-done), kind=kOutput, calls=%fused_computation.11 | convolution fusion | flops 7461370880 | bytes 39720960 | tf_op jit(solution)/shard_map/dot_general | solution.py:51
  337.2 13.0 %convert_element_type.113 = bf16[32,196,768]{2,1,0:T(8,128)(2,1)} reshape(bf16[6272,768]{1,0:T(8,128)(2,1)} %convolution_convert_fusion) | data formatting | bytes 19267584 | tf_op jit(solution)/shard_map/convert_element_type | solution.py:166
  351.5 14.5 %convolution_convert_fusion.1 = bf16[6272,768]{1,0:T(8,128)(2,1)} fusion(bf16[6272,768]{1,0:T(8,128)(2,1)} %get-tuple-element.89, bf16[768,768]{0,1:T(8,128)(2,1)S(1)} %copy-done.46), kind=kOutput, calls=%fused_computation.30 | convolution fusion | flops 7403569152 | bytes 20447232 | tf_op jit(solution)/shard_map/dot_general | solution.py:41
  366.0 13.3 %convert_element_type.108 = bf16[32,196,768]{2,1,0:T(8,128)(2,1)} reshape(bf16[6272,768]{1,0:T(8,128)(2,1)} %convolution_convert_fusion.1) | data formatting | bytes 19267584 | tf_op jit(solution)/shard_map/convert_element_type | solution.py:147
  379.3 13.2 %dot_general.74 = bf16[32,196,768]{2,1,0:T(8,128)(2,1)} reshape(bf16[6272,768]{1,0:T(8,128)(2,1)} %copy-done.7) | data formatting | bytes 19267584 | tf_op jit(solution)/shard_map/dot_general | solution.py:41
  392.5 13.3 %dot_general.77 = bf16[32,196,768]{2,1,0:T(8,128)(2,1)} reshape(bf16[6272,768]{1,0:T(8,128)(2,1)} %get-tuple-element.89) | data formatting | bytes 19267584 | tf_op jit(solution)/shard_map/dot_general | solution.py:41
  405.8 14.1 %convolution_convert_fusion.2 = bf16[768,768]{0,1:T(8,128)(2,1)} fusion(bf16[6272,768]{1,0:T(8,128)(2,1)} %get-tuple-element.89, bf16[6272,768]{1,0:T(8,128)(2,1)} %reshape.127), kind=kOutput, calls=%fused_computation.114 | convolution fusion | flops 7399342080 | bytes 20447232 | tf_op jit(solution)/shard_map/dot_general | solution.py:45
  459.8 14.2 %convolution_convert_fusion.3 = bf16[768,768]{1,0:T(8,128)(2,1)} fusion(bf16[6272,768]{1,0:T(8,128)(2,1)} %reshape.126, bf16[6272,768]{1,0:T(8,128)(2,1)} %copy-done.7), kind=kOutput, calls=%fused_computation.115 | convolution fusion | flops 7399342080 | bytes 20447232 | tf_op jit(solution)/shard_map/dot_general | solution.py:45
  474.0 39.6 %reduce-scatter.7.cloned.1.call-done = bf16[8,196,768]{2,1,0:T(8,128)(2,1)} async-done(((bf16[32,196,768]{2,1,0:T(8,128)(2,1)}), bf16[8,196,768]{2,1,0:T(8,128)(2,1)}) %reduce-scatter.7.cloned.1.call-update) | async-done | bytes 2408464 | tf_op jit(solution)/shard_map/reduce_scatter | solution.py:146
  608.4 10.5 %fusion.46 = f32[8,196,768]{2,1,0:T(8,128)S(1)} fusion(f32[8,768,196]{1,2,0:T(8,128)} %get-tuple-element.91, f32[8,196]{1,0:T(8,128)S(1)} %broadcast_multiply_fusion, f32[8,196]{1,0:T(8,128)S(1)} %broadcast_multiply_fusion.1, f32[8,196]{1,0:T(8,128)S(1)} %copy-done.17, f32[768]{0:T(1024)S(1)} %copy-done.35, f32[8,196]{1,0:T(8,128)S(1)} %copy-done.31, ...), kind=kLoop, calls=%fused_computation.82 | loop fusion | flops 24084480 | bytes 19354752 | tf_op jit(solution)/shard_map/add | solution.py:203
  622.6 60.6 %all-reduce = (f32[2,768]{1,0:T(2,128)}, f32[2,768]{1,0:T(2,128)}, f32[384]{0:T(512)}, f32[196]{0:T(256)}, f32[3072]{0:T(1024)}, /*index=5*/f32[768]{0:T(1024)}) all-reduce(f32[2,768]{1,0:T(2,128)S(1)} %fusion.104, f32[2,768]{1,0:T(2,128)S(1)} %fusion.102, f32[384]{0:T(512)S(1)} %get-tuple-element.92, ...), channel_id=1, replica_groups=mesh['dp'=8,'mp'=4] {'dp','mp'}, use_global_device_ids=true, to_apply=%region_18.0 | all-reduce | flops 7492 | bytes 59936 | tf_op jit(solution)/shard_map/psum | solution.py:226
  692.0 23.2 %all-reduce.3.cloned.1.call-done = f32[2,196,48]{1,2,0:T(8,128)} async-done(((f32[2,196,48]{1,2,0:T(8,128)}), f32[2,196,48]{1,2,0:T(8,128)}) %all-reduce.3.cloned.1.call-update) | async-done | bytes 75280 | tf_op jit(solution)/shard_map/psum | solution.py:225
  715.3 65.3 %reduce-scatter.11.cloned.1.call-done = f32[8,256]{1,0:T(8,128)} async-done(((f32[64,256]{1,0:T(8,128)}), f32[8,256]{1,0:T(8,128)}) %reduce-scatter.11.cloned.1.call-update) | async-done | bytes 8208 | tf_op jit(solution)/shard_map/reduce_scatter | solution.py:219
  (215 shorter events, 194.4 us)
Async XLA Ops:
  7.2 146.5 %all-gather.5.cloned.1.call-start = ((), (), s32[]{:S(2)}) async-start(), calls=%async_computation.8 | async-start | bytes 12042240 | tf_op jit(solution)/shard_map/all_gather | solution.py:141
  7.9 80.5 %copy-start.16 = (f32[8,196]{1,0:T(8,128)}, f32[8,196]{1,0:T(8,128)S(1)}, u32[]{:S(2)}) copy-start(f32[8,196]{1,0:T(8,128)S(1)} %convert_element_type.99) | copy-start | bytes 18820
  10.3 47.5 %copy-start.28 = (f32[8,196]{1,0:T(8,128)}, f32[8,196]{1,0:T(8,128)S(1)}, u32[]{:S(2)}) copy-start(f32[8,196]{1,0:T(8,128)S(1)} %broadcast_multiply_fusion.5) | copy-start | bytes 18820
  13.8 69.0 %copy-start.26 = (f32[768]{0:T(1024)}, f32[768]{0:T(1024)S(1)}, u32[]{:S(2)}) copy-start(f32[768]{0:T(1024)S(1)} %get-tuple-element.72) | copy-start | bytes 9220
  87.1 109.9 %all-gather.7.cloned.1.call-start = ((), (), s32[]{:S(2)}) async-start(), calls=%async_computation.9 | async-start | bytes 1327104 | tf_op jit(solution)/shard_map/all_gather | solution.py:116
  87.9 174.8 %all-gather.11.cloned.1.call-start = ((), (), s32[]{:S(2)}) async-start(), calls=%async_computation.12 | async-start | bytes 12042240 | tf_op jit(solution)/shard_map/all_gather | solution.py:152
  88.3 78.3 %copy-start.36 = (f32[8]{0:T(128)}, f32[8]{0:T(128)S(1)}, u32[]{:S(2)}) copy-start(f32[8]{0:T(128)S(1)} %convert_reduce_fusion.9) | copy-start | bytes 100
  91.3 214.5 %all-gather.9.cloned.1.call-start = ((), (), s32[]{:S(2)}) async-start(), calls=%async_computation.10 | async-start | bytes 1327104 | tf_op jit(solution)/shard_map/all_gather | solution.py:117
  92.1 381.9 %reduce-scatter.9.cloned.1.call-start = ((), (), s32[]{:S(2)}) async-start(), calls=%async_computation.13 | async-start | bytes 12288000 | tf_op jit(solution)/shard_map/reduce_scatter | solution.py:165
  350.3 163.4 %reduce-scatter.7.cloned.1.call-start = ((), (), s32[]{:S(2)}) async-start(), calls=%async_computation.11 | async-start | bytes 12288000 | tf_op jit(solution)/shard_map/reduce_scatter | solution.py:146
  419.9 120.8 %all-to-all-start.2 = ((bf16[8,768,96]{1,2,0:T(8,128)(2,1)}), bf16[8,768,96]{1,2,0:T(8,128)(2,1)}, u32[]{:S(2)}, u32[]{:S(2)}) async-start(bf16[8,768,96]{1,2,0:T(8,128)(2,1)} %bitcast.16), calls=%async_computation.4 | async-start | bytes 2359296 | tf_op jit(solution)/shard_map/all_to_all | solution.py:16
  424.2 154.6 %reduce-scatter.13.cloned.1.call-start = ((), (), s32[]{:S(2)}) async-start(), calls=%async_computation.16 | async-start | bytes 655360 | tf_op jit(solution)/shard_map/reshape | solution.py:213
  459.7 53.9 %copy-start.11 = (f32[8,768]{1,0:T(8,128)S(1)}, f32[8,768]{1,0:T(8,128)}, u32[]{:S(2)}) copy-start(f32[8,768]{1,0:T(8,128)} %copy-done.10) | copy-start | bytes 73732
  459.7 53.9 %copy-start.15 = (f32[8,196]{1,0:T(8,128)S(1)}, f32[8,196]{1,0:T(8,128)}, u32[]{:S(2)}) copy-start(f32[8,196]{1,0:T(8,128)} %copy-done.14) | copy-start | bytes 18820
  459.7 53.9 %copy-start.17 = (f32[8,196]{1,0:T(8,128)S(1)}, f32[8,196]{1,0:T(8,128)}, u32[]{:S(2)}) copy-start(f32[8,196]{1,0:T(8,128)} %copy-done.16) | copy-start | bytes 18820
  459.7 53.9 %copy-start.21 = (f32[8,196]{1,0:T(8,128)S(1)}, f32[8,196]{1,0:T(8,128)}, u32[]{:S(2)}) copy-start(f32[8,196]{1,0:T(8,128)} %copy-done.20) | copy-start | bytes 18820
  459.7 53.9 %copy-start.27 = (f32[768]{0:T(1024)S(1)}, f32[768]{0:T(1024)}, u32[]{:S(2)}) copy-start(f32[768]{0:T(1024)} %copy-done.26) | copy-start | bytes 9220
  459.8 53.9 %copy-start.38 = (f32[768]{0:T(1024)S(1)}, f32[768]{0:T(1024)}, u32[]{:S(2)}) copy-start(f32[768]{0:T(1024)} %param.26) | copy-start | bytes 9220
  474.0 46.0 %copy-start.4 = (bf16[8,196,768]{2,1,0:T(8,128)(2,1)S(1)}, bf16[8,196,768]{2,1,0:T(8,128)(2,1)}, u32[]{:S(2)}) copy-start(bf16[8,196,768]{2,1,0:T(8,128)(2,1)} %reduce-scatter.9.cloned.1.call-done) | copy-start | bytes 7225348
  540.7 34.2 %all-to-all-start.1 = ((bf16[8,96,768]{2,1,0:T(8,128)(2,1)}), bf16[8,96,768]{2,1,0:T(8,128)(2,1)}, u32[]{:S(2)}, u32[]{:S(2)}) async-start(bf16[8,96,768]{2,1,0:T(8,128)(2,1)} %bitcast.118), calls=%async_computation.3 | async-start | bytes 2359296 | tf_op jit(solution)/shard_map/all_to_all | solution.py:16
  574.9 22.8 %all-to-all-start = ((bf16[8,2,196,48]{2,3,1,0:T(8,128)(2,1)}), bf16[8,2,196,48]{2,3,1,0:T(8,128)(2,1)S(1)}, u32[]{:S(2)}, u32[]{:S(2)}) async-start(bf16[8,2,196,48]{2,3,1,0:T(8,128)(2,1)} %copy.65), calls=%async_computation.2 | async-start | bytes 786432 | tf_op jit(solution)/shard_map/all_to_all | solution.py:16
  597.7 86.3 %all-to-all-start.3 = ((bf16[8,8,20272]{2,0,1:T(8,128)(2,1)}), bf16[8,8,20272]{2,0,1:T(8,128)(2,1)}, u32[]{:S(2)}, u32[]{:S(2)}) async-start(bf16[8,8,20272]{2,0,1:T(8,128)(2,1)} %copy.69), calls=%async_computation.5 | async-start | bytes 5210112 | tf_op jit(solution)/shard_map/all_to_all | solution.py:217
  603.7 111.6 %all-reduce.3.cloned.1.call-start = ((), (), s32[]{:S(2)}) async-start(), calls=%async_computation.14 | async-start | bytes 196608 | tf_op jit(solution)/shard_map/psum | solution.py:225
  683.9 96.6 %reduce-scatter.11.cloned.1.call-start = ((), (), s32[]{:S(2)}) async-start(), calls=%async_computation.15 | async-start | bytes 73728 | tf_op jit(solution)/shard_map/reduce_scatter | solution.py:219
  (45 other events, 515.1 us)
Sparse Core Ops, SparseCore 0:
  87.2 66.4 all-gather.4
  155.9 41.0 all-gather.6
  198.6 64.1 all-gather.10
  264.8 41.0 all-gather.8
  350.4 79.7 reduce-scatter.8
  432.7 80.9 reduce-scatter.6
  516.1 21.6 reduce-scatter.12
  684.0 31.1 all-reduce.2
  719.2 61.2 reduce-scatter.10
where the time goes:
time: 795 us; the launch traced here: 789 us
  waiting for transfers between devices  248 us (31%)
  matrix products  189 us (24%)
  local copies, waits for them, and re-layouts  156 us (20%)
  blocking collectives  93.3 us (12%)
  other arithmetic  66.6 us (8%)
  starting transfers between devices  20.3 us (3%)
  between operations  15.3 us (2%)
    dot_general x6, matrix products, matmul(): return jnp.dot(left, right, preferred_element_type=jnp.float32)  85.2 us
    reduce_scatter x1, waiting for transfers between devices, body(): lax.psum_scatter(partial_scores, 'dp', scatter_dimension=0, tiled=True)  65.3 us
    all_gather x1, waiting for transfers between devices, body(): second_group = lax.all_gather(second, 'mp', axis=0, tiled=True)  60.8 us
    psum x1, blocking collectives, body(): lax.psum((jnp.sum(gain_each, axis=0), jnp.sum(shift_each, axis=0), jnp.su...  60.6 us
    reduce_scatter x1, waiting for transfers between devices, body(): lax.psum_scatter(partial_out.reshape(-1, patches, features).astype(jnp.bf...  39.6 us
    dot_general x3, matrix products, contract_cols(): lax.dot_general(left, right, (((1,), (1,)), ((), ())), preferred_element_...  34.9 us
    all_gather x1, blocking collectives, body(): lax.all_gather(token_weights.astype(jnp.bfloat16), 'dp', axis=2, tiled=True)  32.7 us
    unnamed x124, local copies, waits for them, and re-layouts  30 us
  transfers between devices with their start and end apart: 13, of which 8 were waited for; matrix products, arithmetic and copies ran while one was open for 40% of the time, Pallas kernels for 0%

commit v1 on v0

v1 whole, which is shorter than its diff:
```python
import functools

import jax
import jax.numpy as jnp
from jax import lax
from jax.experimental import pallas as pl
from jax.experimental.pallas import tpu as pltpu
from jax.sharding import PartitionSpec as P

norm_eps = 1e-06
bf16 = jnp.bfloat16
f32 = jnp.float32
vmem_cap = 56 * 1024 * 1024


def dot(left, right):
    return jnp.dot(left, right, preferred_element_type=f32)


def dot_nt(left, right):
    return lax.dot_general(left, right, (((1,), (1,)), ((), ())), preferred_element_type=f32)


def dot_tn(left, right):
    return lax.dot_general(left, right, (((0,), (0,)), ((), ())), preferred_element_type=f32)


def gelu_pair(values):
    reach = jnp.abs(values)
    ratio = 1.0 / (1.0 + 0.23164188 * reach)
    bell = jnp.exp2(values * values * -0.7213475204444817)
    series = 0.5307027145
    series = series * ratio - 0.7265760135
    series = series * ratio + 0.7107068705
    series = series * ratio - 0.142248368
    series = series * ratio + 0.127414796
    tail = series * ratio * bell
    cumulative = jnp.where(values >= 0.0, 1.0 - tail, tail)
    return (values * cumulative, cumulative + values * bell * 0.3989422804014327)


def normalize(values):
    average = jnp.mean(values, axis=-1, keepdims=True)
    centered = values - average
    spread = jnp.mean(centered * centered, axis=-1, keepdims=True)
    inverse = lax.rsqrt(spread + norm_eps)
    return (centered * inverse, inverse)


def norm_back(grad_norm, normed, inverse):
    first_mean = jnp.mean(grad_norm, axis=-1, keepdims=True)
    second_mean = jnp.mean(grad_norm * normed, axis=-1, keepdims=True)
    return inverse * (grad_norm - first_mean - normed * second_mean)


def token_forward_kernel(
    image_ref, keep_ref, inward_t_ref, outward_ref, gain_ref, shift_ref, mixing_ref, patch_ref, width_ref,
    hidden_ref, slope_ref, second_ref, normed_ref, inverse_ref, pooled_ref, left_ref,
):
    inputs = image_ref[0].astype(f32)
    keep = keep_ref[0]
    normed_one, _ = normalize(inputs)
    masked = ((normed_one * gain_ref[0:1] + shift_ref[0:1]) * keep).astype(bf16)
    mixed = dot(inward_t_ref[...], masked) + mixing_ref[...]
    hidden, slope = gelu_pair(mixed)
    hidden = hidden.astype(bf16)
    hidden_ref[0] = hidden
    slope_ref[0] = slope.astype(bf16)
    residual = inputs + dot(outward_ref[...], hidden) + patch_ref[...]
    pooled_ref[0] = jnp.sum(residual * keep, axis=0, keepdims=True)
    normed_two, inverse_two = normalize(residual)
    second = (normed_two * gain_ref[1:2] + shift_ref[1:2]).astype(bf16)
    second_ref[0] = second
    normed_ref[0] = normed_two.astype(bf16)
    inverse_ref[0] = inverse_two
    left_ref[0] = dot(second, width_ref[...])


def whole(shape):
    return pl.BlockSpec(shape, lambda i: (0,) * len(shape))


def each(shape):
    return pl.BlockSpec((1,) + shape, lambda i: (i,) + (0,) * len(shape))


def token_forward(images, keep, inward_t, outward, norm_gain, norm_bias, mixing_col, patch_col, width_map):
    count, patches, features = images.shape
    mixers = inward_t.shape[0]
    rank = width_map.shape[1]
    return pl.pallas_call(
        token_forward_kernel,
        grid=(count,),
        in_specs=[
            each((patches, features)), each((patches, 1)), whole((mixers, patches)), whole((patches, mixers)),
            whole((2, features)), whole((2, features)), whole((mixers, 1)), whole((patches, 1)), whole((features, rank)),
        ],
        out_specs=[
            each((mixers, features)), each((mixers, features)), each((patches, features)), each((patches, features)),
            each((patches, 1)), each((1, features)), each((patches, rank)),
        ],
        out_shape=[
            jax.ShapeDtypeStruct((count, mixers, features), bf16),
            jax.ShapeDtypeStruct((count, mixers, features), bf16),
            jax.ShapeDtypeStruct((count, patches, features), bf16),
            jax.ShapeDtypeStruct((count, patches, features), bf16),
            jax.ShapeDtypeStruct((count, patches, 1), f32),
            jax.ShapeDtypeStruct((count, 1, features), f32),
            jax.ShapeDtypeStruct((count, patches, rank), f32),
        ],
        compiler_params=pltpu.CompilerParams(vmem_limit_bytes=vmem_cap),
        name="token_forward",
    )(images, keep, inward_t, outward, norm_gain, norm_bias, mixing_col, patch_col, width_map)


def channel_kernel(
    blocks, second_ref, keep_ref, back_ref, left_ref, widen_ref, bias_ref, hidden_map_ref,
    grad_ref, pooled_ref, sum_ref, adapter_ref, share_ref, total_ref,
):
    step = pl.program_id(0)
    second = second_ref[0]
    keep = keep_ref[0]
    hidden_size = widen_ref.shape[1]
    width = hidden_size // blocks

    @pl.when(step == 0)
    def _():
        total_ref[...] = jnp.zeros_like(total_ref)
        sum_ref[...] = jnp.zeros_like(sum_ref)

    grad = None
    right = None
    for block in range(blocks):
        cols = slice(block * width, (block + 1) * width)
        widen = widen_ref[:, cols]
        pre = dot(second, widen) + bias_ref[:, cols]
        hidden, slope = gelu_pair(pre)
        hidden = hidden.astype(bf16).astype(f32)
        pooled_ref[0, :, cols] = jnp.sum(hidden * keep, axis=0, keepdims=True)
        pre_grad = (slope * back_ref[0, :, cols] * keep).astype(bf16)
        sum_ref[:, cols] += jnp.sum(pre_grad.astype(f32), axis=0, keepdims=True)
        part = dot_nt(pre_grad, widen)
        grad = part if grad is None else grad + part
        part = dot_nt(pre_grad, hidden_map_ref[:, cols])
        right = part if right is None else right + part
        total_ref[:, cols] += dot_tn(second, pre_grad)
    grad_ref[0] = grad
    adapter_ref[0] = lax.dot_general(
        left_ref[0], right, (((0,), (0,)), ((), ())), precision=lax.Precision.HIGHEST, preferred_element_type=f32
    )

    @pl.when(step == pl.num_programs(0) - 1)
    def _():
        share_ref[...] = total_ref[...].astype(bf16)


def channel(second, keep, back_rows, left, widen, bias_row, hidden_map_t):
    count, patches, features = second.shape
    hidden_size = widen.shape[1]
    rank = left.shape[2]
    once = pl.Buffered(1)
    return pl.pallas_call(
        functools.partial(channel_kernel, 4),
        grid=(count,),
        in_specs=[
            each((patches, features)), each((patches, 1)), each((1, hidden_size)), each((patches, rank)),
            pl.BlockSpec((features, hidden_size), lambda i: (0, 0), pipeline_mode=once),
            whole((1, hidden_size)), whole((rank, hidden_size)),
        ],
        out_specs=[
            each((patches, features)), each((1, hidden_size)), whole((1, hidden_size)), each((rank, rank)),
            pl.BlockSpec((features, hidden_size), lambda i: (0, 0), pipeline_mode=once),
        ],
        out_shape=[
            jax.ShapeDtypeStruct((count, patches, features), f32),
            jax.ShapeDtypeStruct((count, 1, hidden_size), f32),
            jax.ShapeDtypeStruct((1, hidden_size), f32),
            jax.ShapeDtypeStruct((count, rank, rank), f32),
            jax.ShapeDtypeStruct((features, hidden_size), bf16),
        ],
        scratch_shapes=[pltpu.VMEM((features, hidden_size), f32)],
        compiler_params=pltpu.CompilerParams(vmem_limit_bytes=vmem_cap),
        name="channel",
    )(second, keep, back_rows, left, widen, bias_row, hidden_map_t)


def token_backward_kernel(
    image_ref, keep_ref, row_ref, grad_ref, normed_ref, inverse_ref, hidden_ref, slope_ref,
    inward_ref, outward_t_ref, gain_ref, shift_ref,
    image_grad_ref, vector_ref, sums_ref, patch_ref, total_ref,
):
    step = pl.program_id(0)
    patches, features = image_ref.shape[1:]
    mixers = hidden_ref.shape[1]
    keep = keep_ref[0]
    grad = grad_ref[0]
    normed_two = normed_ref[0].astype(f32)
    half = features // 2
    residual_grad = keep * row_ref[0] + norm_back(grad * gain_ref[1:2], normed_two, inverse_ref[0])
    gain_two = jnp.sum(grad * normed_two, axis=0, keepdims=True)
    shift_two = jnp.sum(grad, axis=0, keepdims=True)
    low = residual_grad.astype(bf16)
    outward_grad = dot_nt(low, hidden_ref[0])
    mixed_grad = (dot(outward_t_ref[...], low) * slope_ref[0].astype(f32)).astype(bf16)
    mixing = dot_nt(jnp.ones((8, features), bf16), mixed_grad)[0:1]
    normed_one, inverse_one = normalize(image_ref[0].astype(f32))
    masked = ((normed_one * gain_ref[0:1] + shift_ref[0:1]) * keep).astype(bf16)
    inward_grad = dot_nt(masked, mixed_grad)
    first_grad = dot(inward_ref[...], mixed_grad) * keep
    gain_one = jnp.sum(first_grad * normed_one, axis=0, keepdims=True)
    shift_one = jnp.sum(first_grad, axis=0, keepdims=True)
    image_grad_ref[0] = residual_grad + norm_back(first_grad * gain_ref[0:1], normed_one, inverse_one)
    vector_ref[0, 0:patches] = inward_grad.astype(bf16)
    vector_ref[0, patches : 2 * patches] = outward_grad.astype(bf16)
    rows = [mixing]
    for row in (gain_one, gain_two, shift_one, shift_two):
        for at in range(0, features, mixers):
            rows.append(row[:, at : at + mixers])
    small = jnp.concatenate(rows, axis=0)
    vector_ref[0, 2 * patches : 2 * patches + len(rows)] = small.astype(bf16)

    @pl.when(step == 0)
    def _():
        total_ref[...] = jnp.zeros_like(total_ref)
        sums_ref[...] = jnp.zeros_like(sums_ref)
        patch_ref[...] = jnp.zeros_like(patch_ref)

    total_ref[0] += inward_grad
    total_ref[1] += outward_grad
    sums_ref[...] += small
    patch_ref[...] += jnp.sum(low.astype(f32), axis=1, keepdims=True)


def token_backward(images, keep, rows, grad, normed, inverse, hidden, slope, inward, outward_t, norm_gain, norm_bias):
    count, patches, features = images.shape
    mixers = hidden.shape[1]
    small = 1 + 4 * (features // mixers)
    return pl.pallas_call(
        token_backward_kernel,
        grid=(count,),
        in_specs=[
            each((patches, features)), each((patches, 1)), each((1, features)), each((patches, features)),
            each((patches, features)), each((patches, 1)), each((mixers, features)), each((mixers, features)),
            whole((patches, mixers)), whole((mixers, patches)), whole((2, features)), whole((2, features)),
        ],
        out_specs=[
            each((patches, features)), each((2 * patches + small, mixers)), whole((small, mixers)), whole((patches, 1)),
            whole((2, patches, mixers)),
        ],
        out_shape=[
            jax.ShapeDtypeStruct((count, patches, features), f32),
            jax.ShapeDtypeStruct((count, 2 * patches + small, mixers), bf16),
            jax.ShapeDtypeStruct((small, mixers), f32),
            jax.ShapeDtypeStruct((patches, 1), f32),
            jax.ShapeDtypeStruct((2, patches, mixers), f32),
        ],
        compiler_params=pltpu.CompilerParams(vmem_limit_bytes=vmem_cap),
        name="token_backward",
    )(images, keep, rows, grad, normed, inverse, hidden, slope, inward, outward_t, norm_gain, norm_bias)


def score_kernel(received_ref, query_ref, score_ref):
    step = pl.program_id(0)
    rows = received_ref.shape[0]
    width = received_ref.shape[2]

    @pl.when(step == 0)
    def _():
        score_ref[...] = jnp.zeros_like(score_ref)

    total = None
    for row in range(rows):
        part = dot_nt(received_ref[row], query_ref[:, row * width : (row + 1) * width])
        total = part if total is None else total + part
    score_ref[...] += total


def scores(received, queries, step_rows):
    rows, count, width = received.shape
    asked = queries.shape[0]
    return pl.pallas_call(
        score_kernel,
        grid=(rows // step_rows,),
        in_specs=[
            pl.BlockSpec((step_rows, count, width), lambda i: (i, 0, 0)),
            pl.BlockSpec((asked, step_rows * width), lambda i: (0, i)),
        ],
        out_specs=whole((count, asked)),
        out_shape=jax.ShapeDtypeStruct((count, asked), f32),
        compiler_params=pltpu.CompilerParams(vmem_limit_bytes=vmem_cap),
        name="scores",
    )(received, queries)


def body(
    images,
    kept_mask,
    pooled_grad,
    token_weights,
    norm_gain,
    norm_bias,
    mixing_bias,
    patch_bias,
    widening,
    narrowing,
    hidden_bias,
    output_bias,
    width_maps,
    hidden_maps,
    queries,
):
    count, patches, features = images.shape
    mixers = mixing_bias.shape[0]
    rank = width_maps.shape[2]
    hidden_size = hidden_bias.shape[0]
    groups = lax.axis_size("dp")
    group = lax.axis_index("dp")
    share = queries.shape[1]
    asked = queries.shape[0]

    token_low = lax.all_gather(
        jnp.swapaxes(token_weights, 1, 2).astype(bf16), "dp", axis=1, tiled=True
    )
    widen_own = lax.all_gather(widening.astype(bf16), "dp", axis=0, tiled=True)
    widen = lax.all_gather(widen_own, "mp", axis=1, tiled=True)
    narrow_own = lax.all_gather(narrowing.astype(bf16), "dp", axis=1, tiled=True)
    hidden_map_t = lax.all_gather(hidden_maps[0].T, "mp", axis=1, tiled=True)

    keep_f = kept_mask.astype(f32)
    kept_count = jnp.sum(keep_f, axis=1, keepdims=True)
    keep = keep_f[:, :, None]
    grad_rows = pooled_grad / kept_count
    grad_low = grad_rows.astype(bf16)
    grad_group = lax.all_gather(grad_low, "mp", axis=0, tiled=True)
    back_part = dot_nt(grad_group, narrow_own)
    back_rows = lax.all_to_all(back_part.astype(bf16), "mp", split_axis=0, concat_axis=1, tiled=True).astype(f32)

    inward_t, outward_t = (token_low[0], token_low[1])
    hidden, slope, second, normed, inverse, pooled_in, left = token_forward(
        images, keep, inward_t, outward_t.T, norm_gain, norm_bias, mixing_bias[:, None], patch_bias[:, None], width_maps[0]
    )
    second_grad, chan_pooled, hidden_sum, adapter_in, widen_share = channel(
        second, keep, back_rows[:, None, :], left, widen, hidden_bias[None, :], hidden_map_t
    )
    image_grad, vector, small_sums, patch_sum, token_sum = token_backward(
        images, keep, grad_rows[:, None, :], second_grad, normed, inverse, hidden, slope,
        inward_t.T, outward_t, norm_gain, norm_bias,
    )

    chan_group = lax.all_to_all(
        chan_pooled[:, 0].astype(bf16), "mp", split_axis=1, concat_axis=0, tiled=True
    )
    pooled_part = dot(chan_group, jnp.concatenate([narrow_own, hidden_maps[1]], axis=1))
    pooled_back = lax.psum_scatter(pooled_part, "mp", scatter_dimension=0, tiled=True)
    pooled = (pooled_in[:, 0] + pooled_back[:, :features]) / kept_count + output_bias
    adapter_out = pooled_back[:, features:, None] * dot(grad_low, width_maps[1])[:, None, :]

    chan_all = lax.all_gather(chan_group, "dp", axis=0, tiled=True)
    grad_all = lax.all_to_all(grad_group, "dp", split_axis=1, concat_axis=0, tiled=True)
    narrowing_grad = dot_tn(chan_all, grad_all)

    widen_mine = lax.psum_scatter(widen_share, "mp", scatter_dimension=1, tiled=True)
    widening_grad = lax.psum_scatter(widen_mine, "dp", scatter_dimension=0, tiled=True).astype(f32)

    token_mine = lax.psum_scatter(token_sum.astype(bf16), "dp", scatter_dimension=2, tiled=True)
    token_grad = lax.psum(token_mine.astype(f32), "mp")

    row_ends = [-(-share * (place + 1) // mixers) for place in range(groups)]
    row_starts = [share * place // mixers for place in range(groups)]
    part_rows = max(end - start for start, end in zip(row_starts, row_ends))
    adapter_rows = jnp.concatenate(
        [adapter_in.reshape(count, rank * rank), adapter_out.reshape(count, rank * rank)], axis=1
    ).astype(bf16)
    whole_rows = row_starts[-1] + part_rows
    fill = (whole_rows - vector.shape[1]) * mixers - adapter_rows.shape[1]
    adapter_rows = jnp.pad(adapter_rows, ((0, 0), (0, fill))).reshape(count, -1, mixers)
    rows_first = jnp.swapaxes(jnp.concatenate([vector, adapter_rows], axis=1), 0, 1)
    parts = jnp.stack([rows_first[start : start + part_rows] for start in row_starts], axis=0)
    received = lax.all_to_all(parts, "dp", split_axis=0, concat_axis=2, tiled=True)[0]
    offset = group * share - mixers * (group * share // mixers)
    shifted = lax.dynamic_update_slice(
        jnp.zeros((asked, part_rows * mixers), bf16), queries, (jnp.int32(0), offset.astype(jnp.int32))
    )
    step_rows = max(step for step in range(1, 10) if part_rows % step == 0)
    partial_scores = scores(received, shifted, step_rows)
    influence = lax.psum_scatter(partial_scores, "dp", scatter_dimension=0, tiled=True)

    small, patch_grad, hidden_grad, output_grad = lax.psum(
        (
            small_sums,
            patch_sum[:, 0],
            hidden_sum[0],
            jnp.sum(grad_low.astype(f32) * kept_count, axis=0),
        ),
        ("dp", "mp"),
    )
    lines = features // mixers
    mixing_grad = small[0]
    gain_grad = small[1 : 1 + 2 * lines].reshape(2, features)
    shift_grad = small[1 + 2 * lines :].reshape(2, features)
    return (
        pooled,
        image_grad,
        token_grad,
        gain_grad,
        shift_grad,
        mixing_grad,
        patch_grad,
        widening_grad,
        narrowing_grad,
        hidden_grad,
        output_grad,
        influence,
    )


def solution(mesh):
    placed = (
        P(("dp", "mp"), None, None),
        P(("dp", "mp"), None),
        P(("dp", "mp"), None),
        P(None, None, "dp"),
        P(),
        P(),
        P(),
        P(),
        P("dp", "mp"),
        P("mp", "dp"),
        P(),
        P(),
        P(),
        P(None, "mp", None),
        P(None, "dp"),
    )
    return jax.shard_map(
        body,
        mesh=mesh,
        in_specs=placed,
        out_specs=(
            P(("dp", "mp"), None),
            P(("dp", "mp"), None, None),
            P(None, None, "dp"),
            P(),
            P(),
            P(),
            P(),
            P("dp", "mp"),
            P("mp", "dp"),
            P(),
            P(),
            P(("dp", "mp"), None),
        ),
        check_vma=False,
    )
```

time: 795 us -> 618 us (0.78)
  matrix products: 189 us -> 4.43 us
  Pallas kernels: 0 us -> 103 us
  other arithmetic: 66.6 us -> 13.1 us
  local copies, waits for them, and re-layouts: 156 us -> 103 us
  blocking collectives: 93.3 us -> 122 us
  waiting for transfers between devices: 248 us -> 236 us
    dot_general x19 -> x4, matrix products: 189 us -> 4.43 us  [the longest x1 2.22 us: dot_nt(): lax.dot_general(left, right, (((1,), (1,)), ((), ())), preferred_element_...]
    pallas_call x0 -> x4, Pallas kernels: none -> 103 us  [the longest x1 57 us: channel(): pl.pallas_call(functools.partial(channel_kernel, 4), grid=(count,), in_sp...]
    unnamed x9 -> x10, waiting for transfers between devices: 0.15 us -> 86.1 us
    all_gather x4 -> x3, waiting for transfers between devices: 110 us -> 47.6 us  [the longest x1 43.9 us: body(): widen_own = lax.all_gather(widening.astype(bf16), 'dp', axis=0, tiled=True)]
    dynamic_update_slice x1, local copies, waits for them, and re-layouts: 0.3 us -> 57.5 us  [body(): lax.dynamic_update_slice(jnp.zeros((asked, part_rows * mixers), bf16), qu...]
    all_gather x1 -> x4, blocking collectives: 32.7 us -> 75.6 us  [the longest x1 31.7 us: body(): lax.all_gather(jnp.swapaxes(token_weights, 1, 2).astype(bf16), 'dp', axis...]
    convert_element_type x7 -> x3, local copies, waits for them, and re-layouts: 40.5 us -> 2.01 us  [the longest x1 1.21 us: body(): token_sum.astype(bf16)]
    dot_general x4 -> x0, local copies, waits for them, and re-layouts: 27.4 us -> none  [the longest x2 26.5 us: matmul(): return jnp.dot(left, right, preferred_element_type=jnp.float32)]
  transfers between devices with their start and end apart: 13 -> 12, of which waited for: 8 -> 7; matrix products, arithmetic and copies ran while one was open for 40% -> 19% of each run, Pallas kernels for 0% -> 5%
where the time goes in v1:
time: 618 us; the launch traced here: 614 us
  waiting for transfers between devices  236 us (38%)
  blocking collectives  122 us (20%)
  local copies, waits for them, and re-layouts  103 us (17%)
  Pallas kernels  103 us (17%)
  starting transfers between devices  17.3 us (3%)
  between operations  15.8 us (3%)
  other arithmetic  13.1 us (2%)
    unnamed x10, waiting for transfers between devices  86.1 us
    reduce_scatter x1, waiting for transfers between devices, body(): lax.psum_scatter(partial_scores, 'dp', scatter_dimension=0, tiled=True)  58.3 us
    dynamic_update_slice x1, local copies, waits for them, and re-layouts, body(): lax.dynamic_update_slice(jnp.zeros((asked, part_rows * mixers), bf16), qu...  57.5 us
    pallas_call x1, Pallas kernels, channel(): pl.pallas_call(functools.partial(channel_kernel, 4), grid=(count,), in_sp...  57 us
    psum x1, blocking collectives, body(): lax.psum((small_sums, patch_sum[:, 0], hidden_sum[0], jnp.sum(grad_low.as...  45.9 us
    all_gather x1, waiting for transfers between devices, body(): widen_own = lax.all_gather(widening.astype(bf16), 'dp', axis=0, tiled=True)  43.9 us
    reduce_scatter x1, waiting for transfers between devices, body(): lax.psum_scatter(widen_share, 'mp', scatter_dimension=1, tiled=True)  41.4 us
    all_gather x1, blocking collectives, body(): lax.all_gather(jnp.swapaxes(token_weights, 1, 2).astype(bf16), 'dp', axis...  31.7 us
  transfers between devices with their start and end apart: 12, of which 7 were waited for; matrix products, arithmetic and copies ran while one was open for 19% of the time, Pallas kernels for 5%

profile of v1, /device:TPU:0, one launch (start us, length us, event | category | flops | bytes accessed | tf_op | source)
XLA Modules:
  0.0 614.5 jit_solution(12754355266440514240)
XLA Ops:
  10.7 43.9 %all-gather.6.cloned.1.call-done = bf16[768,768]{1,0:T(8,128)(2,1)} async-done(((bf16[96,768]{1,0:T(8,128)(2,1)}), bf16[768,768]{1,0:T(8,128)(2,1)}) %all-gather.6.cloned.1.call-update) | async-done | bytes 1179664 | tf_op jit(solution)/shard_map/all_gather | solution.py:324
  56.4 5.2 all_gather.22
  62.5 31.7 %all_gather.21 = bf16[2,384,196]{2,1,0:T(8,128)(2,1)S(1)} all-gather(bf16[2,48,196]{2,1,0:T(8,128)(2,1)S(1)} %convert_bitcast_fusion.1), channel_id=1, replica_groups=mesh['dp'=8,'mp'=4] {'dp'}, dimensions={1}, use_global_device_ids=true | all-gather | bytes 338688 | tf_op jit(solution)/shard_map/all_gather | solution.py:321
  95.0 3.7 all-gather.4.cloned.1.call-done
  100.9 3.3 all-to-all-start
  104.3 7.6 %all_gather.26.hidden_map_ref = bf16[64,3072]{1,0:T(8,128)(2,1)} all-gather(bf16[64,768]{1,0:T(8,128)(2,1)S(1)} %get-tuple-element.95), channel_id=1, replica_groups=mesh['dp'=8,'mp'=4] {'mp'}, dimensions={1}, use_global_device_ids=true | all-gather | bytes 491520 | tf_op jit(solution)/shard_map/all_gather | solution.py:327
  119.5 19.4 %token_forward.1 = (bf16[8,384,768]{2,1,0:T(8,128)(2,1)}, bf16[8,384,768]{2,1,0:T(8,128)(2,1)}, bf16[8,196,768]{2,1,0:T(8,128)(2,1)}, bf16[8,196,768]{2,1,0:T(8,...) custom-call(bf16[8,196,768]{2,1,0:T(8,128)(2,1)} %copy.56.image_ref, ...), custom_call_target="tpu_custom_call" | custom-call | tf_op jit(solution)/shard_map/token_forward/pallas_call | solution.py:91
  139.8 57.0 %channel.1 = (f32[8,196,768]{2,1,0:T(8,128)}, f32[8,1,3072]{2,1,0:T(1,128)}, f32[1,3072]{1,0:T(1,128)}, f32[8,64,64]{2,1,0:T(8,128)}, bf16[768,3072]{1,0:T(8,128)(2,1)}) custom-call(bf16[8,196,768]{2,1,0:T(8,128)(2,1)} %get-tuple-element.30.second_ref, f32[8,196,1]{2,1,0:T(8,128)} %copy.57.keep_ref, f32[8,1,3072]{2,1,0:T(1,128)} %reshape.74.back_ref, ...), custom_call_target="tpu_custom_call" | custom-call | tf_op jit(solution)/shard_map/channel/pallas_call | solution.py:162
  196.8 17.7 %token_backward.1 = (f32[8,196,768]{2,1,0:T(8,128)}, bf16[8,401,384]{2,1,0:T(8,128)(2,1)}, f32[9,384]{1,0:T(8,128)}, f32[196,1]{1,0:T(8,128)}, f32[2,196,384]{2,1,0:T(8,128)}) custom-call(bf16[8,196,768]{2,1,0:T(8,128)(2,1)} %copy.56.image_ref, f32[8,196,1]{2,1,0:T(8,128)} %copy.57.keep_ref, f32[8,1,768]{2,1,0:T(1,128)} %broadcast_in_dim.27.row_ref, ...), custom_call_target="tpu_custom_call" | custom-call | tf_op jit(solution)/shard_map/token_backward/pallas_call | solution.py:238
  217.8 4.6 all-to-all-start.1
  223.6 2.8 all-to-all-done.1
  227.5 60.4 %all-reduce.8.cloned.1.call-done = bf16[2,196,384]{1,0,2:T(2,128)(2,1)} async-done(((bf16[2,196,384]{1,0,2:T(2,128)(2,1)}), bf16[2,196,384]{1,0,2:T(2,128)(2,1)}) %all-reduce.8.cloned.1.call-update) | async-done | bytes 301072
  290.8 3.7 all-to-all-start.2
  296.1 25.0 %all-reduce.10.cloned.1.call-done = (f32[32,832]{1,0:T(8,128)}, f32[2,196,48]{1,0,2:T(2,128)}) async-done(((f32[32,832]{1,0:T(8,128)}, f32[2,196,48]{1,0,2:T(2,128)}), (f32[32,832]{1,0:T(8,128)}, f32[2,196,48]{1,0,2:T(2,128)})) %all-reduce.10.cloned.1.call-update) | async-done | bytes 181776
  325.3 5.5 all-to-all-start.3
  330.9 41.4 %reduce-scatter.4.cloned.1.call-done = bf16[768,768]{1,0:T(8,128)(2,1)} async-done(((bf16[768,3072]{1,0:T(8,128)(2,1)}), bf16[768,768]{1,0:T(8,128)(2,1)}) %reduce-scatter.4.cloned.1.call-update) | async-done | bytes 1179664 | tf_op jit(solution)/shard_map/reduce_scatter | solution.py:362
  372.3 14.0 %copy.72 = bf16[256,20272]{1,0:T(8,128)(2,1)} copy(bf16[256,20272]{0,1:T(8,128)(2,1)} %param.29) | data formatting | bytes 20758528 | tf_op args[14]
  386.4 4.7 broadcast_in_dim.28
  391.1 57.5 %dynamic_update_slice.3.query_ref = bf16[256,20736]{1,0:T(8,128)(2,1)} dynamic-update-slice(bf16[256,20736]{1,0:T(8,128)(2,1)} %broadcast_in_dim.28, bf16[256,20272]{1,0:T(8,128)(2,1)} %copy.72, s32[]{:T(128)} %constant.9.clone.1, s32[]{:T(128)S(6)} %select_n.9) | dynamic-update-slice | bytes 20758532 | tf_op jit(solution)/shard_map/dynamic_update_slice | solution.py:381
  448.7 6.2 %copy.73 = f32[8,196,768]{2,0,1:T(8,128)} copy(f32[8,196,768]{2,1,0:T(8,128)} %get-tuple-element.71) | data formatting | bytes 9633792
  455.0 45.9 %all-reduce.3 = (f32[9,384]{1,0:T(8,128)S(1)}, f32[196]{0:T(256)}, f32[3072]{0:T(1024)}, f32[768]{0:T(1024)}) all-reduce(f32[9,384]{1,0:T(8,128)S(1)} %copy-done.11, f32[196]{0:T(256)S(1)} %reduce.2, f32[3072]{0:T(1024)S(1)} %bitcast.96, f32[768]{0:T(1024)S(1)} %get-tuple-element.88), channel_id=1, replica_groups=mesh['dp'=8,'mp'=4] {'dp','mp'}, use_global_device_ids=true, to_apply=%region_4.0 | all-reduce | flops 7492 | bytes 59936 | tf_op jit(solution)/shard_map/psum | solution.py:388
  502.8 31.2 %all_gather.27 = bf16[256,768]{1,0:T(8,128)(2,1)S(1)} all-gather(bf16[32,768]{1,0:T(8,128)(2,1)S(1)} %bitcast.94), channel_id=1, replica_groups=mesh['dp'=8,'mp'=4] {'dp'}, dimensions={0}, use_global_device_ids=true | all-gather | bytes 442368 | tf_op jit(solution)/shard_map/all_gather | solution.py:358
  537.7 8.5 %scores.1 = f32[64,256]{1,0:T(8,128)} custom-call(bf16[54,64,384]{2,1,0:T(8,128)(2,1)} %copy_bitcast_fusion.received_ref, bf16[256,20736]{1,0:T(8,128)(2,1)} %dynamic_update_slice.3.query_ref), custom_call_target="tpu_custom_call" | custom-call | tf_op jit(solution)/shard_map/scores/pallas_call | solution.py:281
  549.3 58.3 %reduce-scatter.8.cloned.1.call-done = f32[8,256]{1,0:T(8,128)} async-done(((f32[64,256]{1,0:T(8,128)}), f32[8,256]{1,0:T(8,128)}) %reduce-scatter.8.cloned.1.call-update) | async-done | bytes 8208 | tf_op jit(solution)/shard_map/reduce_scatter | solution.py:386
  (116 shorter events, 39.3 us)
Async XLA Ops:
  7.2 87.0 %copy-start.9 = (s32[8,196]{1,0:T(8,128)S(1)}, s32[8,196]{1,0:T(8,128)}, u32[]{:S(2)}) copy-start(s32[8,196]{1,0:T(8,128)} %param.16) | copy-start | bytes 18820
  7.2 87.0 %copy-start.5 = (bf16[2,768,64]{1,2,0:T(8,128)(2,1)S(1)}, bf16[2,768,64]{1,2,0:T(8,128)(2,1)}, u32[]{:S(2)}) copy-start(bf16[2,768,64]{1,2,0:T(8,128)(2,1)} %param.28) | copy-start | bytes 589828
  7.2 47.4 %all-gather.6.cloned.1.call-start = ((), (), s32[]{:S(2)}) async-start(), calls=%async_computation.8 | async-start | bytes 1327104 | tf_op jit(solution)/shard_map/all_gather | solution.py:324
  9.0 89.8 %all-gather.4.cloned.1.call-start = ((), (), s32[]{:S(2)}) async-start(), calls=%async_computation.7 | async-start | bytes 1327104 | tf_op jit(solution)/shard_map/all_gather | solution.py:326
  10.7 129.1 %all-gather.8.cloned.1.call-start = ((), (), s32[]{:S(2)}) async-start(), calls=%async_computation.9 | async-start | bytes 5898240 | tf_op jit(solution)/shard_map/all_gather | solution.py:325
  54.6 57.3 %copy-start.1 = (bf16[8,196,768]{2,0,1:T(8,128)(2,1)S(1)}, bf16[8,196,768]{2,0,1:T(8,128)(2,1)}, u32[]{:S(2)}) copy-start(bf16[8,196,768]{2,0,1:T(8,128)(2,1)} %param.15) | copy-start | bytes 7225348
  100.9 38.0 %all-to-all-start = ((bf16[4,8,768]{2,1,0:T(8,128)(2,1)}), bf16[4,8,768]{2,1,0:T(8,128)(2,1)S(1)}, u32[]{:S(2)}, u32[]{:S(2)}) async-start(bf16[4,8,768]{2,1,0:T(8,128)(2,1)} %fusion.4), calls=%async_computation | async-start | bytes 98304 | tf_op jit(solution)/shard_map/all_to_all | solution.py:336
  104.2 183.8 %all-reduce.8.cloned.1.call-start = ((), (), s32[]{:S(2)}) async-start(), calls=%async_computation.13 | async-start | bytes 786432
  196.8 20.1 %copy-start.8 = (f32[8,1,3072]{2,1,0:T(1,128)S(1)}, f32[8,1,3072]{2,1,0:T(1,128)}, u32[]{:S(2)}) copy-start(f32[8,1,3072]{2,1,0:T(1,128)} %get-tuple-element.32) | copy-start | bytes 294916
  196.8 25.5 %copy-start.17 = (u32[32]{0:T(128)S(1)}, u32[32]{0:T(128)}, u32[]{:S(2)}) copy-start(u32[32]{0:T(128)} %constant.38) | copy-start | bytes 388
  196.8 29.6 %copy-start.2 = (bf16[768,768]{0,1:T(8,128)(2,1)S(1)}, bf16[768,768]{0,1:T(8,128)(2,1)}, u32[]{:S(2)}) copy-start(bf16[768,768]{0,1:T(8,128)(2,1)} %all-gather.4.cloned.1.call-done) | copy-start | bytes 3538948
  217.8 8.6 %all-to-all-start.1 = ((bf16[8,4,768]{2,0,1:T(8,128)(2,1)}), bf16[8,4,768]{2,0,1:T(8,128)(2,1)S(1)}, u32[]{:S(2)}, u32[]{:S(2)}) async-start(bf16[8,4,768]{2,0,1:T(8,128)(2,1)} %bitcast.42), calls=%async_computation.1 | async-start | bytes 98304 | tf_op jit(solution)/shard_map/all_to_all | solution.py:350
  222.4 98.8 %all-reduce.10.cloned.1.call-start = ((), (), s32[]{:S(2)}) async-start(), calls=%async_computation.14 | async-start | bytes 425984
  289.5 6.4 %copy-start.4 = (f32[8,64,64]{2,1,0:T(8,128)S(1)}, f32[8,64,64]{2,1,0:T(8,128)}, u32[]{:S(2)}) copy-start(f32[8,64,64]{2,1,0:T(8,128)} %get-tuple-element.45) | copy-start | bytes 393220
  289.5 82.7 %reduce-scatter.4.cloned.1.call-start = ((), (), s32[]{:S(2)}) async-start(), calls=%async_computation.10 | async-start | bytes 5898240 | tf_op jit(solution)/shard_map/reduce_scatter | solution.py:362
  289.5 32.7 %copy-start = (bf16[8,401,384]{2,1,0:T(8,128)(2,1)S(1)}, bf16[8,401,384]{2,1,0:T(8,128)(2,1)}, u32[]{:S(2)}) copy-start(bf16[8,401,384]{2,1,0:T(8,128)(2,1)} %get-tuple-element.44) | copy-start | bytes 7391236
  290.8 34.5 %all-to-all-start.2 = ((bf16[32,8,96]{2,0,1:T(8,128)(2,1)}), bf16[32,8,96]{2,0,1:T(8,128)(2,1)S(1)}, u32[]{:S(2)}, u32[]{:S(2)}) async-start(bf16[32,8,96]{2,0,1:T(8,128)(2,1)} %copy.68), calls=%async_computation.4 | async-start | bytes 131072 | tf_op jit(solution)/shard_map/all_to_all | solution.py:359
  325.3 210.3 %all-to-all-start.3 = ((bf16[8,54,8,384]{3,2,1,0:T(8,128)(2,1)}), bf16[8,54,8,384]{3,2,1,0:T(8,128)(2,1)S(1)}, u32[]{:S(2)}, u32[]{:S(2)}) async-start(bf16[8,54,8,384]{3,2,1,0:T(8,128)(2,1)} %copy.70), calls=%async_computation.5 | async-start | bytes 5308416 | tf_op jit(solution)/shard_map/all_to_all | solution.py:379
  330.8 216.8 %reduce-scatter.6.cloned.1.call-start = ((), (), s32[]{:S(2)}) async-start(), calls=%async_computation.11 | async-start | bytes 1327104 | tf_op jit(solution)/shard_map/reduce_scatter | solution.py:363
  372.3 235.4 %reduce-scatter.8.cloned.1.call-start = ((), (), s32[]{:S(2)}) async-start(), calls=%async_computation.12 | async-start | bytes 73728 | tf_op jit(solution)/shard_map/reduce_scatter | solution.py:386
  448.7 6.3 %copy-start.12 = (f32[1,3072]{1,0:T(1,128)S(1)}, f32[1,3072]{1,0:T(1,128)}, u32[]{:S(2)}) copy-start(f32[1,3072]{1,0:T(1,128)} %get-tuple-element.43) | copy-start | bytes 36868
  448.7 86.2 %copy-start.7 = (f32[2,196,48]{1,0,2:T(2,128)S(1)}, f32[2,196,48]{1,0,2:T(2,128)}, u32[]{:S(2)}) copy-start(f32[2,196,48]{1,0,2:T(2,128)} %get-tuple-element.87) | copy-start | bytes 225796
  537.7 8.5 %copy-start.10 = (f32[8,1,768]{2,1,0:T(1,128)S(1)}, f32[8,1,768]{2,1,0:T(1,128)}, u32[]{:S(2)}) copy-start(f32[8,1,768]{2,1,0:T(1,128)} %get-tuple-element.29) | copy-start | bytes 73732
  537.7 8.5 %copy-start.13 = (f32[768]{0:T(1024)S(1)}, f32[768]{0:T(1024)}, u32[]{:S(2)}) copy-start(f32[768]{0:T(1024)} %param.26) | copy-start | bytes 9220
  (7 other events, 38.0 us)
Sparse Core Ops, SparseCore 0:
  10.8 43.7 all-gather.5
  57.3 41.3 all-gather.3
  100.3 36.9 all-gather.7
  217.0 70.9 all-reduce.7
  290.9 30.1 all-reduce.9
  323.5 48.6 reduce-scatter.3
  376.0 64.6 reduce-scatter.5
  546.3 61.2 reduce-scatter.7
